TPU v7x, 32 devices: a whole 2x2x4 slice. The times are simulated.
32 devices in a mesh: dp: 2 (over core), context: 16 (over z, y, x).
Axes of the slice: x: 2, y: 2, z: 4, core: 2. Of those that a mesh axis runs over, the one named last changes fastest.
Arguments:
- queries: bfloat16 [2, 2048, 4096], P('dp', 'context'), may hold values from -5 to 5
- keys: bfloat16 [2, 2048, 1024], P('dp', 'context'), may hold values from -5 to 5
- values: bfloat16 [2, 2048, 1024], P('dp', 'context'), may hold values from -5 to 5
- d_proj: bfloat16 [2, 2048, 2048], P('dp', 'context'), may hold values from -5 to 5
- out_weight: bfloat16 [4096, 2048], P('context'), may hold values from -0.09375 to 0.09375
- random_blocks: int32 [32, 15], replicated, may hold values from 1 to 15, as said below
Outputs:
- attn_out: bfloat16 [2, 2048, 4096], P('dp', 'context')
- d_queries: bfloat16 [2, 2048, 4096], P('dp', 'context')
- d_keys: bfloat16 [2, 2048, 1024], P('dp', 'context')
- d_values: bfloat16 [2, 2048, 1024], P('dp', 'context')
- d_out_weight: float32 [4096, 2048], P('context')
Inputs may be any that keep to these rules, and one draw needn't show every extreme that they name: random_blocks[h, i - 1] is the random key block of query block i of head h; it is never i - 1, i or i + 1.
All inputs are finite; a program needn't handle non-finite values.
Results may differ from a plain program's by a relative error of at most 0.03.
Values may be sent and summed in bfloat16 or wider, within the bound.
A program may use at most 192 MiB of HBM per device.

v0:
```python
import functools

import jax
import jax.numpy as jnp
from jax import lax
from jax.experimental import pallas as pl
from jax.experimental.pallas import tpu as pltpu
from jax.sharding import PartitionSpec as P

DH = 128
BLOCK = 128
MESH = pl.DeviceIdType.MESH
F32 = jnp.float32
BF16 = jnp.bfloat16


def greet(n, m):
    me = lax.axis_index("context")
    sequence = lax.axis_index("dp")
    barrier = pltpu.get_barrier_semaphore()
    for step in range(1, n):
        pl.semaphore_signal(
            barrier, inc=1, device_id=(sequence, lax.rem(me + step, n)), device_id_type=MESH
        )
    for step in range(1, m):
        pl.semaphore_signal(
            barrier, inc=1, device_id=(lax.rem(sequence + step, m), me), device_id_type=MESH
        )
    pl.semaphore_wait(barrier, n - 1 + m - 1)


def spread(n, local_heads, group, q_ref, k_ref, v_ref, g_ref, qa_ref, ka_ref, va_ref, ga_ref,
           own_sem, a2a_send, a2a_recv, far_send, far_recv, mid_send, mid_recv, last_send, last_recv):
    rows = q_ref.shape[0]
    me = lax.axis_index("context")
    sequence = lax.axis_index("dp")
    planes = n // 4
    plane = me // 4
    place = lax.rem(me, 4)
    other_x = plane * 4 + place + 1 - 2 * lax.rem(place, 2)
    other_y = plane * 4 + lax.rem(place + 2, 4)
    half = g_ref.shape[1] // 2
    width = local_heads * DH
    greet(n, 1)

    def remote(src, dst, send, recv, device):
        return pltpu.make_async_remote_copy(
            src_ref=src, dst_ref=dst, send_sem=send, recv_sem=recv,
            device_id=(sequence, device), device_id_type=MESH,
        )

    def forward(block, low, send, recv, device, src=None):
        cols = pl.ds(low, half)
        source = ga_ref.at[block, :, cols] if src is None else src.at[:, cols]
        return remote(source, ga_ref.at[block, :, cols], send, recv, device)

    def columns(device):
        kv = (device * local_heads) // group
        return (
            pl.ds(pl.multiple_of(device * width, DH), width),
            pl.ds(pl.multiple_of(kv * DH, DH), DH),
        )

    mine = pl.ds(pl.multiple_of(me * rows, rows), rows)
    waits = []
    for step in range(1, planes):
        copy = remote(g_ref, ga_ref.at[me], far_send.at[step], far_recv.at[step],
                      lax.rem(plane + step, planes) * 4 + place)
        copy.start()
        waits.append(copy)

    def pass_on(step, src=None):
        block = lax.rem(plane + planes - step, planes) * 4 + place
        one = forward(block, 0, mid_send.at[0, step], mid_recv.at[0, step], other_x, src)
        two = forward(block, half, mid_send.at[1, step], mid_recv.at[1, step], other_y, src)
        thr = forward(block, 0, last_send.at[0, step], last_recv.at[0, step], other_y, src)
        fou = forward(block, half, last_send.at[1, step], last_recv.at[1, step], other_x, src)
        out = [one, two, thr, fou]
        for copy in out:
            copy.start()
        return out

    mids = [pass_on(0, g_ref)]
    qc, kc = columns(me)
    own = [
        pltpu.make_async_copy(g_ref, ga_ref.at[me], own_sem.at[0]),
        pltpu.make_async_copy(q_ref.at[:, qc], qa_ref.at[mine, :], own_sem.at[1]),
        pltpu.make_async_copy(k_ref.at[:, kc], ka_ref.at[mine, :], own_sem.at[2]),
        pltpu.make_async_copy(v_ref.at[:, kc], va_ref.at[mine, :], own_sem.at[3]),
    ]
    for copy in own:
        copy.start()
    for step in range(1, n):
        device = lax.rem(me + step, n)
        qc, kc = columns(device)
        for kind, (src, dst, cols) in enumerate(
            ((q_ref, qa_ref, qc), (k_ref, ka_ref, kc), (v_ref, va_ref, kc))
        ):
            copy = remote(src.at[:, cols], dst.at[mine, :],
                          a2a_send.at[kind, step], a2a_recv.at[kind, step], device)
            copy.start()
            waits.append(copy)
    for step in range(1, planes):
        waits[step - 1].wait_recv()
        mids.append(pass_on(step))
    for step in range(planes):
        base = lax.rem(plane + planes - step, planes) * 4
        from_x = base + place + 1 - 2 * lax.rem(place, 2)
        from_y = base + lax.rem(place + 2, 4)
        mids[step][0].wait_recv()
        five = forward(from_x, 0, last_send.at[2, step], last_recv.at[2, step], other_y)
        five.start()
        mids[step][1].wait_recv()
        six = forward(from_y, half, last_send.at[3, step], last_recv.at[3, step], other_x)
        six.start()
        mids[step] += [five, six]
    for step in range(planes):
        for which in range(2, 6):
            mids[step][which].wait_recv()
        for copy in mids[step]:
            copy.wait_send()
    for number, copy in enumerate(waits):
        if number >= planes - 1:
            copy.wait_recv()
        copy.wait_send()
    for copy in own:
        copy.wait()


def attend(local_heads, chosen_ref, q_ref, k_ref, v_ref, g_ref, o_ref, dq_ref, dk_ref, dv_ref,
           dk_acc, dv_acc):
    length = q_ref.shape[0]
    blocks = length // BLOCK
    scaling = DH ** (-0.5)
    dk_acc[...] = jnp.zeros_like(dk_acc)
    dv_acc[...] = jnp.zeros_like(dv_acc)

    def nt(a, b):
        return lax.dot_general(a, b, (((1,), (1,)), ((), ())), preferred_element_type=F32)

    def nn(a, b):
        return lax.dot_general(a, b, (((1,), (0,)), ((), ())), preferred_element_type=F32)

    def tn(a, b):
        return lax.dot_general(a, b, (((0,), (0,)), ((), ())), preferred_element_type=F32)

    def at(block):
        return pl.ds(pl.multiple_of(block * BLOCK, BLOCK), BLOCK)

    def stacked(ref, block):
        rows = ref[at(block), :]
        return jnp.concatenate([rows[:, h * DH:(h + 1) * DH] for h in range(local_heads)], axis=0)

    def unstack(ref, block, value):
        ref[at(block), :] = jnp.concatenate(
            [value[h * BLOCK:(h + 1) * BLOCK] for h in range(local_heads)], axis=1
        ).astype(BF16)

    q = stacked(q_ref, 0)
    g = stacked(g_ref, 0)
    s = nt(q, k_ref[...]) * scaling
    e = jnp.exp(s - jnp.max(s, axis=1, keepdims=True))
    p = e * (1.0 / jnp.sum(e, axis=1, keepdims=True))
    pb = p.astype(BF16)
    o = nn(pb, v_ref[...]).astype(BF16)
    unstack(o_ref, 0, o)
    row_dot = jnp.sum(g.astype(F32) * o.astype(F32), axis=1, keepdims=True)
    ds = (p * (nt(g, v_ref[...]) - row_dot)).astype(BF16)
    unstack(dq_ref, 0, nn(ds, k_ref[...]) * scaling)
    dk_acc[...] += tn(ds, q)
    dv_acc[...] += tn(pb, g)

    def body(i, carry):
        right = jnp.minimum(i + 1, blocks - 1)
        near = [0, i - 1, i, right]
        picked = [chosen_ref[h, i - 1] for h in range(local_heads)]
        q = stacked(q_ref, i)
        g = stacked(g_ref, i)
        kn = jnp.concatenate([k_ref[at(b), :] for b in near], axis=0)
        vn = jnp.concatenate([v_ref[at(b), :] for b in near], axis=0)
        kr = [k_ref[at(b), :] for b in picked]
        vr = [v_ref[at(b), :] for b in picked]

        def per_head(op, a, b):
            return jnp.concatenate(
                [op(a[h * BLOCK:(h + 1) * BLOCK], b[h]) for h in range(local_heads)], axis=0
            )

        sn = nt(q, kn) * scaling
        s1 = jnp.where(i >= 2, sn[:, BLOCK:2 * BLOCK], -jnp.inf)
        s3 = jnp.where(i <= blocks - 2, sn[:, 3 * BLOCK:], -jnp.inf)
        s = jnp.concatenate(
            [sn[:, :BLOCK], s1, sn[:, 2 * BLOCK:3 * BLOCK], s3, per_head(nt, q, kr) * scaling], axis=1
        )
        e = jnp.exp(s - jnp.max(s, axis=1, keepdims=True))
        p = e * (1.0 / jnp.sum(e, axis=1, keepdims=True))
        pb = p.astype(BF16)
        pn, pr = pb[:, :4 * BLOCK], pb[:, 4 * BLOCK:]
        o = (nn(pn, vn) + per_head(nn, pr, vr)).astype(BF16)
        unstack(o_ref, i, o)
        row_dot = jnp.sum(g.astype(F32) * o.astype(F32), axis=1, keepdims=True)
        dp = jnp.concatenate([nt(g, vn), per_head(nt, g, vr)], axis=1)
        ds = (p * (dp - row_dot)).astype(BF16)
        dn, dr = ds[:, :4 * BLOCK], ds[:, 4 * BLOCK:]
        unstack(dq_ref, i, (nn(dn, kn) + per_head(nn, dr, kr)) * scaling)
        dkn = tn(dn, q)
        dvn = tn(pn, g)
        for slot, b in enumerate(near):
            dk_acc[at(b), :] += dkn[slot * BLOCK:(slot + 1) * BLOCK]
            dv_acc[at(b), :] += dvn[slot * BLOCK:(slot + 1) * BLOCK]
        for h in range(local_heads):
            rows = slice(h * BLOCK, (h + 1) * BLOCK)
            dk_acc[at(picked[h]), :] += tn(dr[rows], q[rows])
            dv_acc[at(picked[h]), :] += tn(pr[rows], g[rows])
        return carry

    lax.fori_loop(1, blocks, body, 0)
    dk_ref[...] = (dk_acc[...] * scaling).astype(BF16)
    dv_ref[...] = dv_acc[...].astype(BF16)


def bring_back(n, m, kv_heads, o_ref, dq_ref, dk_ref, dv_ref, w_ref, oo_ref, dqo_ref, dko_ref, dvo_ref,
               dw_ref, k_parts, v_parts, w_parts, own_sem, send, recv, w_send, w_recv):
    rows = oo_ref.shape[0]
    width = o_ref.shape[1]
    me = lax.axis_index("context")
    sequence = lax.axis_index("dp")
    greet(n, m)
    cols = pl.ds(pl.multiple_of(me * width, DH), width)
    w_copies = []
    for step in range(1, m):
        copy = pltpu.make_async_remote_copy(
            src_ref=w_ref, dst_ref=w_parts.at[sequence], send_sem=w_send.at[step],
            recv_sem=w_recv.at[step], device_id=(lax.rem(sequence + step, m), me), device_id_type=MESH,
        )
        copy.start()
        w_copies.append(copy)
    pairs = (
        (o_ref, oo_ref.at[:, cols]),
        (dq_ref, dqo_ref.at[:, cols]),
        (dk_ref, k_parts.at[me]),
        (dv_ref, v_parts.at[me]),
    )
    copies = []
    for step in range(1, n):
        device = lax.rem(me + step, n)
        theirs = pl.ds(pl.multiple_of(device * rows, rows), rows)
        for kind, (src, dst) in enumerate(pairs):
            copy = pltpu.make_async_remote_copy(
                src_ref=src.at[theirs, :], dst_ref=dst, send_sem=send.at[kind, step],
                recv_sem=recv.at[kind, step], device_id=(sequence, device), device_id_type=MESH,
            )
            copy.start()
            copies.append(copy)
    mine = pl.ds(pl.multiple_of(me * rows, rows), rows)
    own = [
        pltpu.make_async_copy(src.at[mine, :], dst, own_sem.at[kind])
        for kind, (src, dst) in enumerate(pairs)
    ]
    own.append(pltpu.make_async_copy(w_ref, w_parts.at[sequence], own_sem.at[4]))
    for copy in own:
        copy.start()
    own[4].wait()
    for copy in w_copies:
        copy.wait()
    tile = 32

    @pl.loop(0, w_ref.shape[0] // tile)
    def _(t):
        at = pl.ds(pl.multiple_of(t * tile, tile), tile)
        total = w_parts[0, at, :].astype(F32)
        for other in range(1, m):
            total = total + w_parts[other, at, :].astype(F32)
        dw_ref[at, :] = total

    for copy in own[:4]:
        copy.wait()
    for copy in copies:
        copy.wait()
    per = n // kv_heads
    for parts, out in ((k_parts, dko_ref), (v_parts, dvo_ref)):
        for kv in range(kv_heads):
            total = parts[kv * per].astype(F32)
            for other in range(1, per):
                total = total + parts[kv * per + other].astype(F32)
            out[:, kv * DH:(kv + 1) * DH] = total.astype(BF16)


def local(queries, keys, values, d_proj, out_weight, random_blocks):
    n = lax.axis_size("context")
    m = lax.axis_size("dp")
    rows = queries.shape[1]
    heads = queries.shape[2] // DH
    kv_heads = keys.shape[2] // DH
    group = heads // kv_heads
    local_heads = heads // n
    width = local_heads * DH
    columns = d_proj.shape[2]
    length = rows * n
    planes = n // 4
    anywhere = pl.BlockSpec(memory_space=pl.ANY)
    vmem = pl.BlockSpec(memory_space=pltpu.VMEM)
    shape = jax.ShapeDtypeStruct
    dma = pltpu.SemaphoreType.DMA

    q_all, k_all, v_all, g_all = pl.pallas_call(
        functools.partial(spread, n, local_heads, group),
        out_shape=(
            shape((length, width), BF16),
            shape((length, DH), BF16),
            shape((length, DH), BF16),
            shape((n, rows, columns), BF16),
        ),
        in_specs=[anywhere] * 4,
        out_specs=(anywhere,) * 4,
        scratch_shapes=[
            dma((4,)),
            dma((3, n)), dma((3, n)),
            dma((planes,)), dma((planes,)),
            dma((2, planes)), dma((2, planes)),
            dma((4, planes)), dma((4, planes)),
        ],
        compiler_params=pltpu.CompilerParams(collective_id=0, has_side_effects=True),
        name="spread",
    )(queries[0], keys[0], values[0], d_proj[0])

    grad_rows = g_all.reshape(length, columns)
    grad_out = lax.dot_general(
        grad_rows, out_weight, (((1,), (1,)), ((), ())), preferred_element_type=F32
    ).astype(BF16)
    chosen = lax.dynamic_slice_in_dim(
        random_blocks, lax.axis_index("context") * local_heads, local_heads, 0
    )
    out, dq, dk, dv = pl.pallas_call(
        functools.partial(attend, local_heads),
        out_shape=(
            shape((length, width), BF16),
            shape((length, width), BF16),
            shape((length, DH), BF16),
            shape((length, DH), BF16),
        ),
        in_specs=[pl.BlockSpec(memory_space=pltpu.SMEM)] + [vmem] * 4,
        out_specs=(vmem,) * 4,
        scratch_shapes=[pltpu.VMEM((length, DH), F32), pltpu.VMEM((length, DH), F32)],
        compiler_params=pltpu.CompilerParams(vmem_limit_bytes=48 * 1024 * 1024),
        name="attend",
    )(chosen, q_all, k_all, v_all, grad_out)
    weight_part = lax.dot_general(
        out, grad_rows, (((0,), (0,)), ((), ())), preferred_element_type=F32
    ).astype(BF16)
    attended, d_queries, d_keys, d_values, d_weight = pl.pallas_call(
        functools.partial(bring_back, n, m, kv_heads),
        out_shape=(
            shape((rows, heads * DH), BF16),
            shape((rows, heads * DH), BF16),
            shape((rows, kv_heads * DH), BF16),
            shape((rows, kv_heads * DH), BF16),
            shape((width, columns), F32),
        ),
        in_specs=[anywhere] * 5,
        out_specs=(anywhere, anywhere, vmem, vmem, vmem),
        scratch_shapes=[
            pltpu.VMEM((n, rows, DH), BF16),
            pltpu.VMEM((n, rows, DH), BF16),
            pltpu.VMEM((m, width, columns), BF16),
            dma((5,)),
            dma((4, n)), dma((4, n)),
            dma((m,)), dma((m,)),
        ],
        compiler_params=pltpu.CompilerParams(
            collective_id=1, has_side_effects=True, vmem_limit_bytes=48 * 1024 * 1024
        ),
        name="bring_back",
    )(out, dq, dk, dv, weight_part)
    return (attended[None], d_queries[None], d_keys[None], d_values[None], d_weight)


def solution(mesh):
    in_specs = (
        P("dp", "context", None),
        P("dp", "context", None),
        P("dp", "context", None),
        P("dp", "context", None),
        P("context", None),
        P(),
    )
    out_specs = (
        P("dp", "context", None),
        P("dp", "context", None),
        P("dp", "context", None),
        P("dp", "context", None),
        P("context", None),
    )
    return jax.shard_map(local, mesh=mesh, in_specs=in_specs, out_specs=out_specs, check_vma=False)
```

profile of v0, /device:TPU:14, one launch (start us, length us, event | category | flops | bytes accessed | tf_op | source)
XLA Modules:
  0.0 239.2 jit_solution(5990155685479009104)
XLA Ops:
  0.6 0.0 copy-start
  0.7 0.9 constant_dynamic-slice_fusion
  1.5 0.1 copy.12.chosen_ref
  1.6 115.0 %spread.1 = (bf16[2048,256]{1,0:T(8,128)(2,1)}, bf16[2048,128]{1,0:T(8,128)(2,1)}, bf16[2048,128]{1,0:T(8,128)(2,1)}, bf16[16,128,2048]{2,1,0:T(8,128)(2,1)}) custom-call(bf16[128,4096]{1,0:T(8,128)(2,1)} %bitcast.19, bf16[128,1024]{1,0:T(8,128)(2,1)} %bitcast.21, bf16[128,1024]{1,0:T(8,128)(2,1)} %bitcast.22, bf16[128,2048]{1,0:T(8,128)(2,1)} %bitcast.20), custom_call_target="tpu_custom_call" | custom-call | tf_op jit(solution)/shard_map/spread/pallas_call | solution.py:306
  116.6 0.0 copy-done
  116.6 0.0 copy-start.1
  116.6 0.0 copy-start.2
  116.6 0.0 copy-start.3
  116.7 6.9 %convolution_convert_fusion.1.g_ref = bf16[2048,256]{1,0:T(8,128)(2,1)} fusion(bf16[2048,2048]{1,0:T(8,128)(2,1)} %bitcast.17, bf16[256,2048]{1,0:T(8,128)(2,1)S(1)} %copy-done), kind=kOutput, calls=%fused_computation.1 | convolution fusion | flops 2148007936 | bytes 10485760 | tf_op jit(solution)/shard_map/dot_general | solution.py:328
  123.5 0.0 copy-done.1
  123.5 0.0 copy-done.2
  123.5 0.0 copy-done.3
  123.5 21.3 %attend.1 = (bf16[2048,256]{1,0:T(8,128)(2,1)S(1)}, bf16[2048,256]{1,0:T(8,128)(2,1)S(1)}, bf16[2048,128]{1,0:T(8,128)(2,1)S(1)}, bf16[2048,128]{1,0:T(8,128)(2,1)S(1)}) custom-call(s32[2,15]{1,0:T(2,128)S(1)} %copy.12.chosen_ref, bf16[2048,256]{1,0:T(8,128)(2,1)S(1)} %copy-done.1, bf16[2048,128]{1,0:T(8,128)(2,1)S(1)} %copy-done.2, ...), custom_call_target="tpu_custom_call" | custom-call | tf_op jit(solution)/shard_map/attend/pallas_call | solution.py:334
  144.9 6.7 %convolution_convert_fusion.w_ref = bf16[256,2048]{1,0:T(8,128)(2,1)} fusion(bf16[2048,256]{1,0:T(8,128)(2,1)S(1)} %get-tuple-element.22.o_ref, bf16[2048,2048]{1,0:T(8,128)(2,1)} %bitcast.18), kind=kOutput, calls=%fused_computation | convolution fusion | flops 2148007936 | bytes 10485760 | tf_op jit(solution)/shard_map/dot_general | solution.py:348
  151.6 81.2 %bring_back.1 = (bf16[128,4096]{1,0:T(8,128)(2,1)S(1)}, bf16[128,4096]{1,0:T(8,128)(2,1)S(1)}, bf16[128,1024]{1,0:T(8,128)(2,1)S(1)}, bf16[128,1024]{1,0:T(8,128)(2,1)S(1)}, f32[256,2048]{1,0:T(8,128)}) custom-call(bf16[2048,256]{1,0:T(8,128)(2,1)S(1)} %get-tuple-element.22.o_ref, bf16[2048,256]{1,0:T(8,128)(2,1)S(1)} %get-tuple-element.23.dq_ref, ...), custom_call_target="tpu_custom_call" | custom-call | tf_op jit(solution)/shard_map/bring_back/pallas_call | solution.py:351
  232.7 1.0 copy.18
  233.7 1.0 copy.19
  234.7 0.7 copy.20
  235.4 0.7 copy.21
  236.1 3.1 %copy.22 = f32[256,2048]{1,0:T(8,128)} copy(f32[256,2048]{1,0:T(8,128)} %get-tuple-element.40) | data formatting | bytes 4194304
Async XLA Ops:
  0.6 116.0 %copy-start = (bf16[256,2048]{1,0:T(8,128)(2,1)S(1)}, bf16[256,2048]{1,0:T(8,128)(2,1)}, u32[]{:S(2)}) copy-start(bf16[256,2048]{1,0:T(8,128)(2,1)} %param.10) | copy-start | bytes 3145732
  116.6 6.9 %copy-start.1 = (bf16[2048,256]{1,0:T(8,128)(2,1)S(1)}, bf16[2048,256]{1,0:T(8,128)(2,1)}, u32[]{:S(2)}) copy-start(bf16[2048,256]{1,0:T(8,128)(2,1)} %get-tuple-element.18.q_ref) | copy-start | bytes 3145732
  116.6 6.9 %copy-start.2 = (bf16[2048,128]{1,0:T(8,128)(2,1)S(1)}, bf16[2048,128]{1,0:T(8,128)(2,1)}, u32[]{:S(2)}) copy-start(bf16[2048,128]{1,0:T(8,128)(2,1)} %get-tuple-element.19.k_ref) | copy-start | bytes 1572868
  116.6 6.9 %copy-start.3 = (bf16[2048,128]{1,0:T(8,128)(2,1)S(1)}, bf16[2048,128]{1,0:T(8,128)(2,1)}, u32[]{:S(2)}) copy-start(bf16[2048,128]{1,0:T(8,128)(2,1)} %get-tuple-element.20.v_ref) | copy-start | bytes 1572868
where the time goes:
time: 239 us
  Pallas kernels  217 us (91%)
  matrix products  13.6 us (6%)
  local copies, waits for them, and re-layouts  7.46 us (3%)
    pallas_call x1, Pallas kernels, local(): pl.pallas_call(functools.partial(spread, n, local_heads, group), out_shap...  115 us
    pallas_call x1, Pallas kernels, local(): pl.pallas_call(functools.partial(bring_back, n, m, kv_heads), out_shape=(...  81.2 us
    pallas_call x1, Pallas kernels, local(): pl.pallas_call(functools.partial(attend, local_heads), out_shape=(shape((...  21.3 us
    dot_general x1, matrix products, local(): lax.dot_general(grad_rows, out_weight, (((1,), (1,)), ((), ())), preferre...  6.88 us
    dot_general x1, matrix products, local(): lax.dot_general(out, grad_rows, (((0,), (0,)), ((), ())), preferred_eleme...  6.7 us
    unnamed x14, local copies, waits for them, and re-layouts  6.6 us

commit v1 on v0

--- a/solution.py
+++ b/solution.py
@@ -29,8 +29,8 @@
     pl.semaphore_wait(barrier, n - 1 + m - 1)
 
 
-def spread(n, local_heads, group, q_ref, k_ref, v_ref, g_ref, qa_ref, ka_ref, va_ref, ga_ref,
-           own_sem, a2a_send, a2a_recv, far_send, far_recv, mid_send, mid_recv, last_send, last_recv):
+def spread(n, local_heads, group, q_ref, k_ref, v_ref, g_ref, w_ref, qa_ref, ka_ref, va_ref, ga_ref,
+           grad_ref, tiles, own_sem, tile_sem, a2a_send, a2a_recv, far_send, far_recv, mid_send, mid_recv, last_send, last_recv):
     rows = q_ref.shape[0]
     me = lax.axis_index("context")
     sequence = lax.axis_index("dp")
@@ -114,16 +114,34 @@
         six = forward(from_y, half, last_send.at[3, step], last_recv.at[3, step], other_x)
         six.start()
         mids[step] += [five, six]
+    own[0].wait()
     for step in range(planes):
         for which in range(2, 6):
             mids[step][which].wait_recv()
+        base = lax.rem(plane + planes - step, planes) * 4
+        loads = [
+            pltpu.make_async_copy(ga_ref.at[base + part], tiles.at[part], tile_sem.at[part])
+            for part in range(4)
+        ]
+        for copy in loads:
+            copy.start()
+        for copy in loads:
+            copy.wait()
+
+        @pl.loop(0, 4)
+        def _(part):
+            at = pl.ds(pl.multiple_of((base + part) * rows, rows), rows)
+            grad_ref[at, :] = lax.dot_general(
+                tiles[part], w_ref[...], (((1,), (1,)), ((), ())), preferred_element_type=F32
+            ).astype(BF16)
+
         for copy in mids[step]:
             copy.wait_send()
     for number, copy in enumerate(waits):
         if number >= planes - 1:
             copy.wait_recv()
         copy.wait_send()
-    for copy in own:
+    for copy in own[1:]:
         copy.wait()
 
 
@@ -219,22 +237,14 @@
     dv_ref[...] = dv_acc[...].astype(BF16)
 
 
-def bring_back(n, m, kv_heads, o_ref, dq_ref, dk_ref, dv_ref, w_ref, oo_ref, dqo_ref, dko_ref, dvo_ref,
-               dw_ref, k_parts, v_parts, w_parts, own_sem, send, recv, w_send, w_recv):
+def bring_back(n, m, kv_heads, o_ref, dq_ref, dk_ref, dv_ref, g_ref, oo_ref, dqo_ref, dko_ref, dvo_ref,
+               dw_ref, k_parts, v_parts, w_own, w_parts, o_vmem, o_turned, g_vmem, own_sem, send, recv, w_send, w_recv):
     rows = oo_ref.shape[0]
     width = o_ref.shape[1]
     me = lax.axis_index("context")
     sequence = lax.axis_index("dp")
     greet(n, m)
     cols = pl.ds(pl.multiple_of(me * width, DH), width)
-    w_copies = []
-    for step in range(1, m):
-        copy = pltpu.make_async_remote_copy(
-            src_ref=w_ref, dst_ref=w_parts.at[sequence], send_sem=w_send.at[step],
-            recv_sem=w_recv.at[step], device_id=(lax.rem(sequence + step, m), me), device_id_type=MESH,
-        )
-        copy.start()
-        w_copies.append(copy)
     pairs = (
         (o_ref, oo_ref.at[:, cols]),
         (dq_ref, dqo_ref.at[:, cols]),
@@ -242,30 +252,66 @@
         (dv_ref, v_parts.at[me]),
     )
     copies = []
-    for step in range(1, n):
-        device = lax.rem(me + step, n)
-        theirs = pl.ds(pl.multiple_of(device * rows, rows), rows)
-        for kind, (src, dst) in enumerate(pairs):
-            copy = pltpu.make_async_remote_copy(
-                src_ref=src.at[theirs, :], dst_ref=dst, send_sem=send.at[kind, step],
-                recv_sem=recv.at[kind, step], device_id=(sequence, device), device_id_type=MESH,
-            )
-            copy.start()
-            copies.append(copy)
+
+    def send_out(kinds):
+        for step in range(1, n):
+            device = lax.rem(me + step, n)
+            theirs = pl.ds(pl.multiple_of(device * rows, rows), rows)
+            for kind in kinds:
+                src, dst = pairs[kind]
+                copy = pltpu.make_async_remote_copy(
+                    src_ref=src.at[theirs, :], dst_ref=dst, send_sem=send.at[kind, step],
+                    recv_sem=recv.at[kind, step], device_id=(sequence, device), device_id_type=MESH,
+                )
+                copy.start()
+                copies.append(copy)
+
+    load_o = pltpu.make_async_copy(o_ref, o_vmem, own_sem.at[4])
+    load_g = pltpu.make_async_copy(g_ref, g_vmem, own_sem.at[5])
+    load_o.start()
+    load_g.start()
+    send_out((0,))
     mine = pl.ds(pl.multiple_of(me * rows, rows), rows)
     own = [
         pltpu.make_async_copy(src.at[mine, :], dst, own_sem.at[kind])
         for kind, (src, dst) in enumerate(pairs)
     ]
-    own.append(pltpu.make_async_copy(w_ref, w_parts.at[sequence], own_sem.at[4]))
+    load_o.wait()
+
+    @pl.loop(0, n)
+    def _(t):
+        at = pl.ds(pl.multiple_of(t * rows, rows), rows)
+        o_turned[:, at] = o_vmem[at, :].T
+
+    load_g.wait()
+    wide = 256
+
+    @pl.loop(0, g_ref.shape[1] // wide)
+    def _(t):
+        at = pl.ds(pl.multiple_of(t * wide, wide), wide)
+        w_own[:, at] = lax.dot_general(
+            o_turned[...], g_vmem[:, at], (((1,), (0,)), ((), ())), preferred_element_type=F32
+        ).astype(BF16)
+
+    w_copies = []
+    for step in range(1, m):
+        copy = pltpu.make_async_remote_copy(
+            src_ref=w_own, dst_ref=w_parts.at[sequence], send_sem=w_send.at[step],
+            recv_sem=w_recv.at[step], device_id=(lax.rem(sequence + step, m), me), device_id_type=MESH,
+        )
+        copy.start()
+        w_copies.append(copy)
+    send_out((1, 2, 3))
     for copy in own:
         copy.start()
-    own[4].wait()
+    to_slot = pltpu.make_async_copy(w_own, w_parts.at[sequence], own_sem.at[6])
+    to_slot.start()
+    to_slot.wait()
     for copy in w_copies:
         copy.wait()
     tile = 32
 
-    @pl.loop(0, w_ref.shape[0] // tile)
+    @pl.loop(0, w_own.shape[0] // tile)
     def _(t):
         at = pl.ds(pl.multiple_of(t * tile, tile), tile)
         total = w_parts[0, at, :].astype(F32)
@@ -303,31 +349,32 @@
     shape = jax.ShapeDtypeStruct
     dma = pltpu.SemaphoreType.DMA
 
-    q_all, k_all, v_all, g_all = pl.pallas_call(
+    q_all, k_all, v_all, g_all, grad_out = pl.pallas_call(
         functools.partial(spread, n, local_heads, group),
         out_shape=(
             shape((length, width), BF16),
             shape((length, DH), BF16),
             shape((length, DH), BF16),
             shape((n, rows, columns), BF16),
+            shape((length, width), BF16),
         ),
-        in_specs=[anywhere] * 4,
-        out_specs=(anywhere,) * 4,
+        in_specs=[anywhere] * 4 + [vmem],
+        out_specs=(anywhere,) * 4 + (vmem,),
         scratch_shapes=[
+            pltpu.VMEM((4, rows, columns), BF16),
+            dma((4,)),
             dma((4,)),
             dma((3, n)), dma((3, n)),
             dma((planes,)), dma((planes,)),
             dma((2, planes)), dma((2, planes)),
             dma((4, planes)), dma((4, planes)),
         ],
-        compiler_params=pltpu.CompilerParams(collective_id=0, has_side_effects=True),
+        compiler_params=pltpu.CompilerParams(
+            collective_id=0, has_side_effects=True, vmem_limit_bytes=56 * 1024 * 1024
+        ),
         name="spread",
-    )(queries[0], keys[0], values[0], d_proj[0])
-
-    grad_rows = g_all.reshape(length, columns)
-    grad_out = lax.dot_general(
-        grad_rows, out_weight, (((1,), (1,)), ((), ())), preferred_element_type=F32
-    ).astype(BF16)
+    )(queries[0], keys[0], values[0], d_proj[0], out_weight)
+
     chosen = lax.dynamic_slice_in_dim(
         random_blocks, lax.axis_index("context") * local_heads, local_heads, 0
     )
@@ -345,9 +392,6 @@
         compiler_params=pltpu.CompilerParams(vmem_limit_bytes=48 * 1024 * 1024),
         name="attend",
     )(chosen, q_all, k_all, v_all, grad_out)
-    weight_part = lax.dot_general(
-        out, grad_rows, (((0,), (0,)), ((), ())), preferred_element_type=F32
-    ).astype(BF16)
     attended, d_queries, d_keys, d_values, d_weight = pl.pallas_call(
         functools.partial(bring_back, n, m, kv_heads),
         out_shape=(
@@ -362,8 +406,12 @@
         scratch_shapes=[
             pltpu.VMEM((n, rows, DH), BF16),
             pltpu.VMEM((n, rows, DH), BF16),
+            pltpu.VMEM((width, columns), BF16),
             pltpu.VMEM((m, width, columns), BF16),
-            dma((5,)),
+            pltpu.VMEM((length, width), BF16),
+            pltpu.VMEM((width, length), BF16),
+            pltpu.VMEM((length, columns), BF16),
+            dma((7,)),
             dma((4, n)), dma((4, n)),
             dma((m,)), dma((m,)),
         ],
@@ -371,7 +419,7 @@
             collective_id=1, has_side_effects=True, vmem_limit_bytes=48 * 1024 * 1024
         ),
         name="bring_back",
-    )(out, dq, dk, dv, weight_part)
+    )(out, dq, dk, dv, g_all.reshape(length, columns))
     return (attended[None], d_queries[None], d_keys[None], d_values[None], d_weight)
 
 

time: 239 us -> 228 us (0.954)
  matrix products: 13.6 us -> 0 us
    dot_general x2 -> x0, matrix products: 13.6 us -> none  [the longest x1 6.88 us: local(): lax.dot_general(grad_rows, out_weight, (((1,), (1,)), ((), ())), preferre...]
    pallas_call x1, Pallas kernels: 115 us -> 121 us  [local(): pl.pallas_call(functools.partial(spread, n, local_heads, group), out_shap...]
    pallas_call x1, Pallas kernels: 81.2 us -> 75.8 us  [local(): pl.pallas_call(functools.partial(bring_back, n, m, kv_heads), out_shape=(...]
    unnamed x14 -> x16, local copies, waits for them, and re-layouts: 6.6 us -> 8.75 us
where the time goes in v1:
time: 228 us; the launch traced here: 227 us
  Pallas kernels  218 us (96%)
  local copies, waits for them, and re-layouts  8.83 us (4%)
    pallas_call x1, Pallas kernels, local(): pl.pallas_call(functools.partial(spread, n, local_heads, group), out_shap...  121 us
    pallas_call x1, Pallas kernels, local(): pl.pallas_call(functools.partial(bring_back, n, m, kv_heads), out_shape=(...  75.8 us
    pallas_call x1, Pallas kernels, local(): pl.pallas_call(functools.partial(attend, local_heads), out_shape=(shape((...  21.3 us
    unnamed x16, local copies, waits for them, and re-layouts  8.75 us

profile of v1, /device:TPU:14, one launch (start us, length us, event | category | flops | bytes accessed | tf_op | source)
XLA Modules:
  0.0 227.2 jit_solution(9357099155804246693)
XLA Ops:
  0.6 0.0 copy-start
  0.7 0.7 copy-done
  1.3 0.1 constant_dynamic-slice_fusion
  1.4 0.1 copy.12.chosen_ref
  1.5 120.6 %spread.1 = (bf16[2048,256]{1,0:T(8,128)(2,1)}, bf16[2048,128]{1,0:T(8,128)(2,1)}, bf16[2048,128]{1,0:T(8,128)(2,1)}, bf16[16,128,2048]{2,1,0:T(8,128)(2,1)}, bf16[2048,256]{1,0:T(8,128)(2,1)}) custom-call(bf16[128,4096]{1,0:T(8,128)(2,1)} %bitcast.14, bf16[128,1024]{1,0:T(8,128)(2,1)} %bitcast.16, bf16[128,1024]{1,0:T(8,128)(2,1)} %bitcast.17, ...), custom_call_target="tpu_custom_call" | custom-call | tf_op jit(solution)/shard_map/spread/pallas_call | solution.py:352
  122.1 0.0 copy-start.1
  122.1 1.2 copy-done.1
  123.3 0.0 copy-start.2
  123.3 1.0 copy-done.2
  124.3 0.0 copy-start.3
  124.3 1.0 copy-done.3
  125.4 21.3 %attend.1 = (bf16[2048,256]{1,0:T(8,128)(2,1)S(1)}, bf16[2048,256]{1,0:T(8,128)(2,1)S(1)}, bf16[2048,128]{1,0:T(8,128)(2,1)S(1)}, bf16[2048,128]{1,0:T(8,128)(2,1)S(1)}) custom-call(s32[2,15]{1,0:T(2,128)S(1)} %copy.12.chosen_ref, bf16[2048,256]{1,0:T(8,128)(2,1)S(1)} %copy-done.1, bf16[2048,128]{1,0:T(8,128)(2,1)S(1)} %copy-done.2, ...), custom_call_target="tpu_custom_call" | custom-call | tf_op jit(solution)/shard_map/attend/pallas_call | solution.py:381
  146.7 75.8 %bring_back.1 = (bf16[128,4096]{1,0:T(8,128)(2,1)S(1)}, bf16[128,4096]{1,0:T(8,128)(2,1)S(1)}, bf16[128,1024]{1,0:T(8,128)(2,1)S(1)}, bf16[128,1024]{1,0:T(8,128)(2,1)S(1)}, f32[256,2048]{1,0:T(8,128)}) custom-call(bf16[2048,256]{1,0:T(8,128)(2,1)S(1)} %get-tuple-element.23.o_ref, bf16[2048,256]{1,0:T(8,128)(2,1)S(1)} %get-tuple-element.24.dq_ref, ...), custom_call_target="tpu_custom_call" | custom-call | tf_op jit(solution)/shard_map/bring_back/pallas_call | solution.py:395
  222.5 1.0 copy.18
  223.5 0.0 copy-start.4
  223.5 1.0 copy.19
  224.4 0.7 copy.20
  225.1 0.7 copy.21
  225.8 0.0 copy-done.4
  225.9 1.3 copy.22
Async XLA Ops:
  0.6 0.7 copy-start
  122.1 1.2 copy-start.1
  123.3 1.0 copy-start.2
  124.3 1.0 copy-start.3
  223.5 2.4 %copy-start.4 = (f32[256,2048]{1,0:T(8,128)S(1)}, f32[256,2048]{1,0:T(8,128)}, u32[]{:S(2)}) copy-start(f32[256,2048]{1,0:T(8,128)} %get-tuple-element.42) | copy-start | bytes 6291460

commit v2 on v1

--- a/solution.py
+++ b/solution.py
@@ -238,7 +238,7 @@
 
 
 def bring_back(n, m, kv_heads, o_ref, dq_ref, dk_ref, dv_ref, g_ref, oo_ref, dqo_ref, dko_ref, dvo_ref,
-               dw_ref, k_parts, v_parts, w_own, w_parts, o_vmem, o_turned, g_vmem, own_sem, send, recv, w_send, w_recv):
+               dw_ref, k_parts, v_parts, own_half, theirs_half, both_half, w_own, w_parts, o_vmem, o_turned, g_vmem, own_sem, send, recv, w_send, w_recv):
     rows = oo_ref.shape[0]
     width = o_ref.shape[1]
     me = lax.axis_index("context")
@@ -248,8 +248,6 @@
     pairs = (
         (o_ref, oo_ref.at[:, cols]),
         (dq_ref, dqo_ref.at[:, cols]),
-        (dk_ref, k_parts.at[me]),
-        (dv_ref, v_parts.at[me]),
     )
     copies = []
 
@@ -268,6 +266,22 @@
 
     load_o = pltpu.make_async_copy(o_ref, o_vmem, own_sem.at[4])
     load_g = pltpu.make_async_copy(g_ref, g_vmem, own_sem.at[5])
+    side = lax.rem(me, 2)
+    pair = me // 2
+    swaps = []
+    for kind, ref in enumerate((dk_ref, dv_ref)):
+        copy = pltpu.make_async_remote_copy(
+            src_ref=ref.at[:, 1 - side], dst_ref=theirs_half.at[kind], send_sem=send.at[2 + kind, 0],
+            recv_sem=recv.at[2 + kind, 0], device_id=(sequence, me + 1 - 2 * side), device_id_type=MESH,
+        )
+        copy.start()
+        swaps.append(copy)
+    halves = [
+        pltpu.make_async_copy(ref.at[:, side], own_half.at[kind], own_sem.at[2 + kind])
+        for kind, ref in enumerate((dk_ref, dv_ref))
+    ]
+    for copy in halves:
+        copy.start()
     load_o.start()
     load_g.start()
     send_out((0,))
@@ -301,7 +315,29 @@
         )
         copy.start()
         w_copies.append(copy)
-    send_out((1, 2, 3))
+    send_out((1,))
+    for copy in swaps + halves:
+        copy.wait()
+
+    @pl.loop(0, n // 2)
+    def _(t):
+        for kind in range(2):
+            both_half[kind, t] = (
+                own_half[kind, t].astype(F32) + theirs_half[kind, t].astype(F32)
+            ).astype(BF16)
+
+    for step in range(1, n // 2):
+        slot = lax.rem(pair + step, n // 2)
+        for kind, parts in enumerate((k_parts, v_parts)):
+            copy = pltpu.make_async_remote_copy(
+                src_ref=both_half.at[kind, slot], dst_ref=parts.at[pair], send_sem=send.at[2 + kind, step],
+                recv_sem=recv.at[2 + kind, step], device_id=(sequence, slot * 2 + side),
+                device_id_type=MESH,
+            )
+            copy.start()
+            copies.append(copy)
+    for kind, parts in enumerate((k_parts, v_parts)):
+        own.append(pltpu.make_async_copy(both_half.at[kind, pair], parts.at[pair], own_sem.at[2 + kind]))
     for copy in own:
         copy.start()
     to_slot = pltpu.make_async_copy(w_own, w_parts.at[sequence], own_sem.at[6])
@@ -319,11 +355,11 @@
             total = total + w_parts[other, at, :].astype(F32)
         dw_ref[at, :] = total
 
-    for copy in own[:4]:
+    for copy in own:
         copy.wait()
     for copy in copies:
         copy.wait()
-    per = n // kv_heads
+    per = n // 2 // kv_heads
     for parts, out in ((k_parts, dko_ref), (v_parts, dvo_ref)):
         for kv in range(kv_heads):
             total = parts[kv * per].astype(F32)
@@ -404,8 +440,11 @@
         in_specs=[anywhere] * 5,
         out_specs=(anywhere, anywhere, vmem, vmem, vmem),
         scratch_shapes=[
-            pltpu.VMEM((n, rows, DH), BF16),
-            pltpu.VMEM((n, rows, DH), BF16),
+            pltpu.VMEM((n // 2, rows, DH), BF16),
+            pltpu.VMEM((n // 2, rows, DH), BF16),
+            pltpu.VMEM((2, n // 2, rows, DH), BF16),
+            pltpu.VMEM((2, n // 2, rows, DH), BF16),
+            pltpu.VMEM((2, n // 2, rows, DH), BF16),
             pltpu.VMEM((width, columns), BF16),
             pltpu.VMEM((m, width, columns), BF16),
             pltpu.VMEM((length, width), BF16),
@@ -419,7 +458,7 @@
             collective_id=1, has_side_effects=True, vmem_limit_bytes=48 * 1024 * 1024
         ),
         name="bring_back",
-    )(out, dq, dk, dv, g_all.reshape(length, columns))
+    )(out, dq, dk.reshape(n // 2, 2, rows, DH), dv.reshape(n // 2, 2, rows, DH), g_all.reshape(length, columns))
     return (attended[None], d_queries[None], d_keys[None], d_values[None], d_weight)
 
 

time: 228 us -> 216 us (0.947)
  Pallas kernels: 218 us -> 205 us
    pallas_call x1, Pallas kernels: 75.8 us -> 63.1 us  [local(): pl.pallas_call(functools.partial(bring_back, n, m, kv_heads), out_shape=(...]
where the time goes in v2:
time: 216 us; the launch traced here: 214 us
  Pallas kernels  205 us (95%)
  local copies, waits for them, and re-layouts  8.83 us (4%)
    pallas_call x1, Pallas kernels, local(): pl.pallas_call(functools.partial(spread, n, local_heads, group), out_shap...  121 us
    pallas_call x1, Pallas kernels, local(): pl.pallas_call(functools.partial(bring_back, n, m, kv_heads), out_shape=(...  63.1 us
    pallas_call x1, Pallas kernels, local(): pl.pallas_call(functools.partial(attend, local_heads), out_shape=(shape((...  21.3 us
    unnamed x16, local copies, waits for them, and re-layouts  8.75 us

profile of v2, /device:TPU:14, one launch (start us, length us, event | category | flops | bytes accessed | tf_op | source)
XLA Modules:
  0.0 214.5 jit_solution(4031867878035818287)
XLA Ops:
  0.6 0.0 copy-start
  0.7 0.7 copy-done
  1.3 0.1 constant_dynamic-slice_fusion
  1.4 0.1 copy.12.chosen_ref
  1.5 120.6 %spread.1 = (bf16[2048,256]{1,0:T(8,128)(2,1)}, bf16[2048,128]{1,0:T(8,128)(2,1)}, bf16[2048,128]{1,0:T(8,128)(2,1)}, bf16[16,128,2048]{2,1,0:T(8,128)(2,1)}, bf16[2048,256]{1,0:T(8,128)(2,1)}) custom-call(bf16[128,4096]{1,0:T(8,128)(2,1)} %bitcast.18, bf16[128,1024]{1,0:T(8,128)(2,1)} %bitcast.20, bf16[128,1024]{1,0:T(8,128)(2,1)} %bitcast.21, ...), custom_call_target="tpu_custom_call" | custom-call | tf_op jit(solution)/shard_map/spread/pallas_call | solution.py:388
  122.1 0.0 copy-start.1
  122.1 1.2 copy-done.1
  123.3 0.0 copy-start.2
  123.3 1.0 copy-done.2
  124.3 0.0 copy-start.3
  124.3 1.0 copy-done.3
  125.4 21.3 %attend.1 = (bf16[2048,256]{1,0:T(8,128)(2,1)S(1)}, bf16[2048,256]{1,0:T(8,128)(2,1)S(1)}, bf16[2048,128]{1,0:T(8,128)(2,1)S(1)}, bf16[2048,128]{1,0:T(8,128)(2,1)S(1)}) custom-call(s32[2,15]{1,0:T(2,128)S(1)} %copy.12.chosen_ref, bf16[2048,256]{1,0:T(8,128)(2,1)S(1)} %copy-done.1, bf16[2048,128]{1,0:T(8,128)(2,1)S(1)} %copy-done.2, ...), custom_call_target="tpu_custom_call" | custom-call | tf_op jit(solution)/shard_map/attend/pallas_call | solution.py:417
  146.7 63.1 %bring_back.1 = (bf16[128,4096]{1,0:T(8,128)(2,1)S(1)}, bf16[128,4096]{1,0:T(8,128)(2,1)S(1)}, bf16[128,1024]{1,0:T(8,128)(2,1)S(1)}, bf16[128,1024]{1,0:T(8,128)(2,1)S(1)}, f32[256,2048]{1,0:T(8,128)}) custom-call(bf16[2048,256]{1,0:T(8,128)(2,1)S(1)} %get-tuple-element.23.o_ref, bf16[2048,256]{1,0:T(8,128)(2,1)S(1)} %get-tuple-element.24.dq_ref, ...), custom_call_target="tpu_custom_call" | custom-call | tf_op jit(solution)/shard_map/bring_back/pallas_call | solution.py:431
  209.8 1.0 copy.18
  210.8 0.0 copy-start.4
  210.8 1.0 copy.19
  211.7 0.7 copy.20
  212.4 0.7 copy.21
  213.1 0.0 copy-done.4
  213.1 1.3 copy.22
Async XLA Ops:
  0.6 0.7 copy-start
  122.1 1.2 copy-start.1
  123.3 1.0 copy-start.2
  124.3 1.0 copy-start.3
  210.8 2.4 %copy-start.4 = (f32[256,2048]{1,0:T(8,128)S(1)}, f32[256,2048]{1,0:T(8,128)}, u32[]{:S(2)}) copy-start(f32[256,2048]{1,0:T(8,128)} %get-tuple-element.42) | copy-start | bytes 6291460
